TPU v7x, 32 devices: a whole 2x2x4 slice. The times are simulated.
32 devices in a mesh: dp: 16 (over z, y, x), chan: 2 (over core).
Axes of the slice: x: 2, y: 2, z: 4, core: 2. Of those that a mesh axis runs over, the one named last changes fastest.
Arguments:
- images: bfloat16 [32, 18, 32, 1024], P('dp', None, None, 'chan'), may hold values from -12 to 12
- extents: int32 [32, 2], P('dp'), may hold values from 5 to 16, as said below
- cotangent: bfloat16 [32, 9, 16, 2048], P('dp', None, None, 'chan'), may hold values from -6 to 6
- reduce1: bfloat16 [1024, 512], P(None, 'chan'), may hold values from -0.1875 to 0.1875
- spatial1: bfloat16 [3, 3, 512, 512], P(None, None, None, 'chan'), may hold values from -0.09375 to 0.09375
- expand1: bfloat16 [512, 2048], P(None, 'chan'), may hold values from -0.25 to 0.25
- shortcut: bfloat16 [1024, 2048], P(None, 'chan'), may hold values from -0.1875 to 0.1875
- reduce2: bfloat16 [2048, 512], P(None, 'chan'), may hold values from -0.125 to 0.125
- spatial2: bfloat16 [3, 3, 512, 512], P(None, None, None, 'chan'), may hold values from -0.09375 to 0.09375
- expand2: bfloat16 [512, 2048], P(None, 'chan'), may hold values from -0.25 to 0.25
- norm_one: float32 [2, 512], P(None, 'chan'), may hold values from -1 to 1.5, as said below
- norm_two: float32 [2, 512], P(None, 'chan'), may hold values from -1 to 1.5, as said below
- norm_three: float32 [2, 2048], P(None, 'chan'), may hold values from -1 to 1.5, as said below
- norm_skip: float32 [2, 2048], P(None, 'chan'), may hold values from -1 to 1.5, as said below
- norm_four: float32 [2, 512], P(None, 'chan'), may hold values from -1 to 1.5, as said below
- norm_five: float32 [2, 512], P(None, 'chan'), may hold values from -1 to 1.5, as said below
- norm_six: float32 [2, 2048], P(None, 'chan'), may hold values from -1 to 1.5, as said below
Outputs:
- block_one: bfloat16 [32, 9, 16, 2048], P('dp', None, None, 'chan')
- block_two: bfloat16 [32, 9, 16, 2048], P('dp', None, None, 'chan')
- input_grad: bfloat16 [32, 18, 32, 1024], P('dp', None, None, 'chan')
- reduce1_grad: float32 [1024, 512], P(None, 'chan')
- spatial1_grad: float32 [3, 3, 512, 512], P(None, None, None, 'chan')
- expand1_grad: float32 [512, 2048], P(None, 'chan')
- shortcut_grad: float32 [1024, 2048], P(None, 'chan')
- reduce2_grad: float32 [2048, 512], P(None, 'chan')
- spatial2_grad: float32 [3, 3, 512, 512], P(None, None, None, 'chan')
- expand2_grad: float32 [512, 2048], P(None, 'chan')
- norm_one_grad: float32 [2, 512], P(None, 'chan')
- norm_two_grad: float32 [2, 512], P(None, 'chan')
- norm_three_grad: float32 [2, 2048], P(None, 'chan')
- norm_skip_grad: float32 [2, 2048], P(None, 'chan')
- norm_four_grad: float32 [2, 512], P(None, 'chan')
- norm_five_grad: float32 [2, 512], P(None, 'chan')
- norm_six_grad: float32 [2, 2048], P(None, 'chan')
Inputs may be any that keep to these rules, and one draw needn't show every extreme that they name: `extents`: column 0 is an image's valid rows, from 5 to 9; column 1 its valid columns, from 8 to 16. The first of the 2 images of each index of dp fills the whole grid. `norm_one`: row 0 lies in 0.5 to 1.5, row 1 in -1 to 1. `norm_two`: row 0 lies in 0.5 to 1.5, row 1 in -1 to 1. `norm_three`: row 0 lies in 0.5 to 1.5, row 1 in -1 to 1. `norm_skip`: row 0 lies in 0.5 to 1.5, row 1 in -1 to 1. `norm_four`: row 0 lies in 0.5 to 1.5, row 1 in -1 to 1. `norm_five`: row 0 lies in 0.5 to 1.5, row 1 in -1 to 1. `norm_six`: row 0 lies in 0.5 to 1.5, row 1 in -1 to 1.
All inputs are finite; a program needn't handle non-finite values.
Results may differ from a plain program's by a relative error of at most 0.025.
Values may be sent and summed in bfloat16 or wider, within the bound.
No kernel may reach another device: no remote copies, remote signals or barrier semaphores. Data moves between devices by JAX's collectives and lax.ppermute only.
A program may use at most 640 MiB of HBM per device.

v0:
```python
import jax
import jax.numpy as jnp
from jax import lax
from jax.sharding import PartitionSpec as P

epsilon = 1e-05


def pixel_masks(extents, row_count, col_count, factor):
    heights = extents[:, 0][:, None, None] * factor
    widths = extents[:, 1][:, None, None] * factor
    row_index = lax.broadcasted_iota(jnp.int32, (1, row_count, col_count), 1)
    col_index = lax.broadcasted_iota(jnp.int32, (1, row_count, col_count), 2)
    return ((row_index < heights) & (col_index < widths)).astype(jnp.float32)


def silu_slope(values):
    logistic = jax.nn.sigmoid(values)
    return logistic * (1.0 + values * (1.0 - logistic))


def spread_in(active):
    return lax.all_gather(active, "chan", axis=3, tiled=True)


def spread_out(partial_sums):
    return lax.psum_scatter(
        partial_sums.astype(jnp.bfloat16), "chan", scatter_dimension=3, tiled=True
    ).astype(jnp.float32)


def dense(active, matrix):
    return jnp.einsum("nhwk,kc->nhwc", active, matrix, preferred_element_type=jnp.float32)


def dense_back(active, matrix, grad_out):
    matrix_grad = jnp.einsum("nhwk,nhwc->kc", active, grad_out, preferred_element_type=jnp.float32)
    input_part = jnp.einsum("nhwc,kc->nhwk", grad_out, matrix, preferred_element_type=jnp.float32)
    return (matrix_grad, input_part)


def tap_slices(tap_row, tap_col, stride, rows_out, cols_out):
    row_slice = slice(tap_row, tap_row + stride * (rows_out - 1) + 1, stride)
    col_slice = slice(tap_col, tap_col + stride * (cols_out - 1) + 1, stride)
    return (row_slice, col_slice)


def spatial(active, kernel, stride):
    rows_out = active.shape[1] // stride
    cols_out = active.shape[2] // stride
    padded = jnp.pad(active, ((0, 0), (1, 1), (1, 1), (0, 0)))
    result = jnp.zeros((active.shape[0], rows_out, cols_out, kernel.shape[3]), jnp.float32)
    for tap_row in range(3):
        for tap_col in range(3):
            row_slice, col_slice = tap_slices(tap_row, tap_col, stride, rows_out, cols_out)
            window = padded[:, row_slice, col_slice, :]
            result = result + jnp.einsum(
                "nhwk,kc->nhwc",
                window,
                kernel[tap_row, tap_col],
                preferred_element_type=jnp.float32,
            )
    return result


def spatial_back(active, kernel, grad_out, stride):
    rows_out = grad_out.shape[1]
    cols_out = grad_out.shape[2]
    padded = jnp.pad(active, ((0, 0), (1, 1), (1, 1), (0, 0)))
    input_part = jnp.zeros(padded.shape, jnp.float32)
    kernel_grads = []
    for tap_row in range(3):
        for tap_col in range(3):
            row_slice, col_slice = tap_slices(tap_row, tap_col, stride, rows_out, cols_out)
            window = padded[:, row_slice, col_slice, :]
            kernel_grads.append(
                jnp.einsum("nhwk,nhwc->kc", window, grad_out, preferred_element_type=jnp.float32)
            )
            contribution = jnp.einsum(
                "nhwc,kc->nhwk",
                grad_out,
                kernel[tap_row, tap_col],
                preferred_element_type=jnp.float32,
            )
            input_part = input_part.at[:, row_slice, col_slice, :].add(contribution)
    kernel_grad = jnp.stack(kernel_grads).reshape(3, 3, kernel.shape[2], kernel.shape[3])
    return (kernel_grad, input_part[:, 1:-1, 1:-1, :])


def normalize(conv_out, pixel_mask, norm_params):
    cells = pixel_mask[..., None]
    first = (jnp.sum(conv_out * cells, axis=(0, 1, 2)), jnp.sum(pixel_mask))
    totals, pixels = lax.psum((first[0], first[1]), "dp")
    average = totals / pixels
    centred = conv_out - average
    second = jnp.sum(centred * centred * cells, axis=(0, 1, 2))
    spread = lax.psum(second, "dp")
    variance = spread / pixels
    inverse = lax.rsqrt(variance + epsilon)
    normed = centred * inverse
    return (norm_params[0] * normed + norm_params[1], normed, inverse, pixels)


def norm_back(grad_pre, normed, inverse, pixels, norm_params, pixel_mask):
    local_sums = (jnp.sum(grad_pre, axis=(0, 1, 2)), jnp.sum(grad_pre * normed, axis=(0, 1, 2)))
    beta_grad, gamma_grad = lax.psum((local_sums[0], local_sums[1]), "dp")
    grad_conv = (
        pixel_mask[..., None]
        * norm_params[0]
        * inverse
        * (grad_pre - (beta_grad + normed * gamma_grad) / pixels)
    )
    return (grad_conv.astype(jnp.bfloat16), jnp.stack([gamma_grad, beta_grad]))


def activate(pre_norm, cells):
    return (jax.nn.silu(pre_norm) * cells).astype(jnp.bfloat16)


def local(
    images,
    extents,
    cotangent,
    reduce1,
    spatial1,
    expand1,
    shortcut,
    reduce2,
    spatial2,
    expand2,
    norm_one,
    norm_two,
    norm_three,
    norm_skip,
    norm_four,
    norm_five,
    norm_six,
):
    inner_mask = pixel_masks(extents, images.shape[1], images.shape[2], 2)
    outer_mask = pixel_masks(extents, cotangent.shape[1], cotangent.shape[2], 1)
    inner_cells = inner_mask[..., None]
    outer_cells = outer_mask[..., None]
    masked_in = images * inner_cells.astype(jnp.bfloat16)
    gathered_x = spread_in(masked_in)
    pre_one, hat_one, inv_one, pix_in = normalize(dense(gathered_x, reduce1), inner_mask, norm_one)
    gathered_one = spread_in(activate(pre_one, inner_cells))
    pre_two, hat_two, inv_two, pix_out = normalize(
        spatial(gathered_one, spatial1, 2), outer_mask, norm_two
    )
    gathered_two = spread_in(activate(pre_two, outer_cells))
    skipped_x = gathered_x[:, 0::2, 0::2, :]
    pre_three, hat_three, inv_three, pix_three = normalize(
        dense(gathered_two, expand1), outer_mask, norm_three
    )
    pre_skip, hat_skip, inv_skip, pix_skip = normalize(
        dense(skipped_x, shortcut), outer_mask, norm_skip
    )
    joined_one = pre_three + pre_skip
    block_one = activate(joined_one, outer_cells)
    gathered_mid = spread_in(block_one)
    pre_four, hat_four, inv_four, pix_four = normalize(
        dense(gathered_mid, reduce2), outer_mask, norm_four
    )
    gathered_four = spread_in(activate(pre_four, outer_cells))
    pre_five, hat_five, inv_five, pix_five = normalize(
        spatial(gathered_four, spatial2, 1), outer_mask, norm_five
    )
    gathered_five = spread_in(activate(pre_five, outer_cells))
    pre_six, hat_six, inv_six, pix_six = normalize(
        dense(gathered_five, expand2), outer_mask, norm_six
    )
    joined_two = pre_six + block_one.astype(jnp.float32)
    block_two = activate(joined_two, outer_cells)
    grad_join2 = cotangent.astype(jnp.float32) * outer_cells * silu_slope(joined_two)
    grad_six, norm_six_grad = norm_back(grad_join2, hat_six, inv_six, pix_six, norm_six, outer_mask)
    expand2_grad, back_five = dense_back(gathered_five, expand2, grad_six)
    grad_five_pre = spread_out(back_five) * outer_cells * silu_slope(pre_five)
    grad_five, norm_five_grad = norm_back(
        grad_five_pre, hat_five, inv_five, pix_five, norm_five, outer_mask
    )
    spatial2_grad, back_four = spatial_back(gathered_four, spatial2, grad_five, 1)
    grad_four_pre = spread_out(back_four) * outer_cells * silu_slope(pre_four)
    grad_four, norm_four_grad = norm_back(
        grad_four_pre, hat_four, inv_four, pix_four, norm_four, outer_mask
    )
    reduce2_grad, back_mid = dense_back(gathered_mid, reduce2, grad_four)
    grad_mid = grad_join2 + spread_out(back_mid)
    grad_join1 = grad_mid * outer_cells * silu_slope(joined_one)
    grad_three, norm_three_grad = norm_back(
        grad_join1, hat_three, inv_three, pix_three, norm_three, outer_mask
    )
    grad_skip, norm_skip_grad = norm_back(
        grad_join1, hat_skip, inv_skip, pix_skip, norm_skip, outer_mask
    )
    expand1_grad, back_two = dense_back(gathered_two, expand1, grad_three)
    shortcut_grad, back_skip = dense_back(skipped_x, shortcut, grad_skip)
    grad_two_pre = spread_out(back_two) * outer_cells * silu_slope(pre_two)
    grad_two, norm_two_grad = norm_back(
        grad_two_pre, hat_two, inv_two, pix_out, norm_two, outer_mask
    )
    spatial1_grad, back_one = spatial_back(gathered_one, spatial1, grad_two, 2)
    grad_one_pre = spread_out(back_one) * inner_cells * silu_slope(pre_one)
    grad_one, norm_one_grad = norm_back(
        grad_one_pre, hat_one, inv_one, pix_in, norm_one, inner_mask
    )
    reduce1_grad, back_x = dense_back(gathered_x, reduce1, grad_one)
    back_x = back_x.at[:, 0::2, 0::2, :].add(back_skip)
    input_grad = (spread_out(back_x) * inner_cells).astype(jnp.bfloat16)
    (
        reduce1_grad,
        spatial1_grad,
        expand1_grad,
        shortcut_grad,
        reduce2_grad,
        spatial2_grad,
        expand2_grad,
    ) = lax.psum(
        (
            reduce1_grad,
            spatial1_grad,
            expand1_grad,
            shortcut_grad,
            reduce2_grad,
            spatial2_grad,
            expand2_grad,
        ),
        "dp",
    )
    return (
        block_one,
        block_two,
        input_grad,
        reduce1_grad,
        spatial1_grad,
        expand1_grad,
        shortcut_grad,
        reduce2_grad,
        spatial2_grad,
        expand2_grad,
        norm_one_grad,
        norm_two_grad,
        norm_three_grad,
        norm_skip_grad,
        norm_four_grad,
        norm_five_grad,
        norm_six_grad,
    )


def solution(mesh):
    return jax.shard_map(
        local,
        mesh=mesh,
        in_specs=(
            P("dp", None, None, "chan"),
            P("dp", None),
            P("dp", None, None, "chan"),
            P(None, "chan"),
            P(None, None, None, "chan"),
            P(None, "chan"),
            P(None, "chan"),
            P(None, "chan"),
            P(None, None, None, "chan"),
            P(None, "chan"),
            P(None, "chan"),
            P(None, "chan"),
            P(None, "chan"),
            P(None, "chan"),
            P(None, "chan"),
            P(None, "chan"),
            P(None, "chan"),
        ),
        out_specs=(
            P("dp", None, None, "chan"),
            P("dp", None, None, "chan"),
            P("dp", None, None, "chan"),
            P(None, "chan"),
            P(None, None, None, "chan"),
            P(None, "chan"),
            P(None, "chan"),
            P(None, "chan"),
            P(None, None, None, "chan"),
            P(None, "chan"),
            P(None, "chan"),
            P(None, "chan"),
            P(None, "chan"),
            P(None, "chan"),
            P(None, "chan"),
            P(None, "chan"),
            P(None, "chan"),
        ),
        check_vma=False,
    )
```

profile of v0, /device:TPU:0, one launch (start us, length us, event | category | flops | bytes accessed | tf_op | source)
XLA Modules:
  0.0 2471.8 jit_solution(14826902269235431775)
XLA Ops:
  27.3 42.6 %all-reduce.11 = (f32[256]{0:T(256)S(1)}, f32[]{:T(128)}) all-reduce(f32[256]{0:T(256)S(1)} %get-tuple-element.295, f32[]{:T(128)} %fusion.158), channel_id=1, replica_groups=mesh['dp'=16,'chan'=2] {'dp'}, use_global_device_ids=true, to_apply=%region_1.0 | all-reduce | flops 257 | bytes 2056 | tf_op jit(solution)/shard_map/psum | solution.py:93
  70.8 36.6 %psum.272 = f32[256]{0:T(256)S(1)} all-reduce(f32[256]{0:T(256)S(1)} %multiply_reduce_fusion.10), channel_id=1, replica_groups=mesh['dp'=16,'chan'=2] {'dp'}, use_global_device_ids=true, to_apply=%region_5.0 | all-reduce | flops 256 | bytes 2048 | tf_op jit(solution)/shard_map/psum | solution.py:97
  211.3 39.2 %all-reduce.10 = (f32[256]{0:T(256)S(1)}, f32[]{:T(128)}) all-reduce(f32[256]{0:T(256)S(1)} %get-tuple-element.297, f32[]{:T(128)} %fusion.178), channel_id=1, replica_groups=mesh['dp'=16,'chan'=2] {'dp'}, use_global_device_ids=true, to_apply=%region_7.8 | all-reduce | flops 257 | bytes 2056 | tf_op jit(solution)/shard_map/psum | solution.py:93
  251.4 36.6 %psum.275 = f32[256]{0:T(256)S(1)} all-reduce(f32[256]{0:T(256)S(1)} %multiply_reduce_fusion.19), channel_id=1, replica_groups=mesh['dp'=16,'chan'=2] {'dp'}, use_global_device_ids=true, to_apply=%region_11.12 | all-reduce | flops 256 | bytes 2048 | tf_op jit(solution)/shard_map/psum | solution.py:97
  292.6 38.6 %psum.276 = f32[1024]{0:T(1024)S(1)} all-reduce(f32[1024]{0:T(1024)S(1)} %get-tuple-element.299), channel_id=1, replica_groups=mesh['dp'=16,'chan'=2] {'dp'}, use_global_device_ids=true, to_apply=%region_13.14 | all-reduce | flops 1024 | bytes 8192 | tf_op jit(solution)/shard_map/psum | solution.py:93
  334.8 36.6 %psum.278 = f32[1024]{0:T(1024)S(1)} all-reduce(f32[1024]{0:T(1024)S(1)} %get-tuple-element.224), channel_id=1, replica_groups=mesh['dp'=16,'chan'=2] {'dp'}, use_global_device_ids=true, to_apply=%region_17.18 | all-reduce | flops 1024 | bytes 8192 | tf_op jit(solution)/shard_map/psum | solution.py:93
  373.5 39.1 %all-reduce.9 = (f32[1024]{0:T(1024)S(1)}, f32[1024]{0:T(1024)S(1)}) all-reduce(f32[1024]{0:T(1024)S(1)} %multiply_reduce_fusion.6, f32[1024]{0:T(1024)S(1)} %get-tuple-element.223), channel_id=1, replica_groups=mesh['dp'=16,'chan'=2] {'dp'}, use_global_device_ids=true, to_apply=%region_19.20 | all-reduce | flops 2048 | bytes 16384 | tf_op jit(solution)/shard_map/psum | solution.py:97
  423.9 42.0 %psum.280 = f32[256]{0:T(256)S(1)} all-reduce(f32[256]{0:T(256)S(1)} %get-tuple-element.302), channel_id=1, replica_groups=mesh['dp'=16,'chan'=2] {'dp'}, use_global_device_ids=true, to_apply=%region_21.22 | all-reduce | flops 256 | bytes 2048 | tf_op jit(solution)/shard_map/psum | solution.py:93
  466.7 36.6 %psum.281 = f32[256]{0:T(256)S(1)} all-reduce(f32[256]{0:T(256)S(1)} %multiply_reduce_fusion.17), channel_id=1, replica_groups=mesh['dp'=16,'chan'=2] {'dp'}, use_global_device_ids=true, to_apply=%region_23.24 | all-reduce | flops 256 | bytes 2048 | tf_op jit(solution)/shard_map/psum | solution.py:97
  510.4 38.6 %psum.282 = f32[256]{0:T(256)S(1)} all-reduce(f32[256]{0:T(256)S(1)} %get-tuple-element.304), channel_id=1, replica_groups=mesh['dp'=16,'chan'=2] {'dp'}, use_global_device_ids=true, to_apply=%region_25.26 | all-reduce | flops 256 | bytes 2048 | tf_op jit(solution)/shard_map/psum | solution.py:93
  549.8 36.6 %psum.283 = f32[256]{0:T(256)S(1)} all-reduce(f32[256]{0:T(256)S(1)} %multiply_reduce_fusion.15), channel_id=1, replica_groups=mesh['dp'=16,'chan'=2] {'dp'}, use_global_device_ids=true, to_apply=%region_27.28 | all-reduce | flops 256 | bytes 2048 | tf_op jit(solution)/shard_map/psum | solution.py:97
  592.6 38.7 %psum.284 = f32[1024]{0:T(1024)S(1)} all-reduce(f32[1024]{0:T(1024)S(1)} %get-tuple-element.306), channel_id=1, replica_groups=mesh['dp'=16,'chan'=2] {'dp'}, use_global_device_ids=true, to_apply=%region_29.30 | all-reduce | flops 1024 | bytes 8192 | tf_op jit(solution)/shard_map/psum | solution.py:93
  633.4 36.8 %psum.285 = f32[1024]{0:T(1024)S(1)} all-reduce(f32[1024]{0:T(1024)S(1)} %multiply_reduce_fusion.4), channel_id=1, replica_groups=mesh['dp'=16,'chan'=2] {'dp'}, use_global_device_ids=true, to_apply=%region_31.32 | all-reduce | flops 1024 | bytes 8192 | tf_op jit(solution)/shard_map/psum | solution.py:97
  674.4 39.1 %all-reduce.8 = (f32[1024]{0:T(1024)S(1)}, f32[1024]{0:T(1024)S(1)}) all-reduce(f32[1024]{0:T(1024)S(1)} %get-tuple-element.216, f32[1024]{0:T(1024)S(1)} %get-tuple-element.215), channel_id=1, replica_groups=mesh['dp'=16,'chan'=2] {'dp'}, use_global_device_ids=true, to_apply=%region_35.36 | all-reduce | flops 2048 | bytes 16384 | tf_op jit(solution)/shard_map/psum | solution.py:106
  722.4 42.0 %all-reduce.7 = (f32[256]{0:T(256)S(1)}, f32[256]{0:T(256)S(1)}) all-reduce(f32[256]{0:T(256)S(1)} %get-tuple-element.222, f32[256]{0:T(256)S(1)} %get-tuple-element.221), channel_id=1, replica_groups=mesh['dp'=16,'chan'=2] {'dp'}, use_global_device_ids=true, to_apply=%region_40.41 | all-reduce | flops 512 | bytes 4096 | tf_op jit(solution)/shard_map/psum | solution.py:106
  821.1 41.9 %all-reduce.6 = (f32[256]{0:T(256)S(1)}, f32[256]{0:T(256)S(1)}) all-reduce(f32[256]{0:T(256)S(1)} %get-tuple-element.220, f32[256]{0:T(256)S(1)} %get-tuple-element.219), channel_id=1, replica_groups=mesh['dp'=16,'chan'=2] {'dp'}, use_global_device_ids=true, to_apply=%region_46.47 | all-reduce | flops 512 | bytes 4096 | tf_op jit(solution)/shard_map/psum | solution.py:106
  875.7 42.5 %all-reduce.5 = (f32[1024]{0:T(1024)S(1)}, f32[1024]{0:T(1024)S(1)}) all-reduce(f32[1024]{0:T(1024)S(1)} %get-tuple-element.213, f32[1024]{0:T(1024)S(1)} %get-tuple-element.214), channel_id=1, replica_groups=mesh['dp'=16,'chan'=2] {'dp'}, use_global_device_ids=true, to_apply=%region_51.52 | all-reduce | flops 2048 | bytes 16384 | tf_op jit(solution)/shard_map/psum | solution.py:106
  928.4 41.8 %all-reduce.4 = (f32[256]{0:T(256)S(1)}, f32[256]{0:T(256)S(1)}) all-reduce(f32[256]{0:T(256)S(1)} %get-tuple-element.218, f32[256]{0:T(256)S(1)} %get-tuple-element.217), channel_id=1, replica_groups=mesh['dp'=16,'chan'=2] {'dp'}, use_global_device_ids=true, to_apply=%region_56.57 | all-reduce | flops 512 | bytes 4096 | tf_op jit(solution)/shard_map/psum | solution.py:106
  1009.8 19.4 scatter_fusion.1
  1048.6 19.4 scatter_fusion.3
  1126.4 19.6 scatter_fusion.7
  1169.1 56.4 %copy.391 = bf16[2,18,32,512]{0,2,1,3:T(8,128)(2,1)} copy(bf16[2,18,32,512]{3,0,2,1:T(2,128)(2,1)} %slice.781) | data formatting | bytes 2359296
  1225.5 107.8 %reshape.596 = bf16[512,1152]{1,0:T(8,128)(2,1)} reshape(bf16[512,18,32,2]{3,2,1,0:T(8,128)(2,1)} %bitcast.223) | data formatting | bytes 2359296
  1344.3 82.8 %reshape.597 = bf16[256,18,32,2]{3,2,1,0:T(8,128)(2,1)} reshape(bf16[256,1152]{1,0:T(8,128)(2,1)} %reduce-scatter.19.cloned.1.call-done) | data formatting | bytes 1179648
  1427.1 36.6 %copy.294 = bf16[2,18,32,256]{3,2,1,0:T(8,128)(2,1)} copy(bf16[2,18,32,256]{0,2,1,3:T(8,128)(2,1)} %bitcast.506) | data formatting | bytes 1179648 | tf_op jit(solution)/shard_map/reduce_scatter | solution.py:27
  1465.5 37.3 %all-reduce.3 = (f32[256]{0:T(256)S(1)}, f32[256]{0:T(256)S(1)}, f32[1024]{0:T(1024)S(1)}) all-reduce(f32[256]{0:T(256)S(1)} %get-tuple-element.211, f32[256]{0:T(256)S(1)} %get-tuple-element.210, f32[1024]{0:T(1024)S(1)} %get-tuple-element.212), channel_id=1, replica_groups=mesh['dp'=16,'chan'=2] {'dp'}, use_global_device_ids=true, to_apply=%region_70.71 | all-reduce | flops 1536 | bytes 12288 | tf_op jit(solution)/shard_map/psum | solution.py:106
  1515.8 20.6 scatter_fusion.9
  1542.1 110.9 %copy.393 = bf16[2,18,32,1024]{0,2,1,3:T(8,128)(2,1)} copy(bf16[2,18,32,1024]{3,0,2,1:T(2,128)(2,1)} %convert_element_type.137) | data formatting | bytes 4718592
  1653.0 213.8 %reshape.598 = bf16[1024,1152]{1,0:T(8,128)(2,1)} reshape(bf16[1024,18,32,2]{3,2,1,0:T(8,128)(2,1)} %bitcast.226) | data formatting | bytes 4718592
  1893.0 164.0 %reshape.599 = bf16[512,18,32,2]{3,2,1,0:T(8,128)(2,1)} reshape(bf16[512,1152]{1,0:T(8,128)(2,1)} %reduce-scatter.21.cloned.1.call-done) | data formatting | bytes 2359296
  2057.0 72.8 %copy.394 = bf16[2,18,32,512]{3,0,2,1:T(2,128)(2,1)S(1)} copy(bf16[2,18,32,512]{0,2,1,3:T(8,128)(2,1)} %bitcast.227) | data formatting | bytes 2359296
  2132.3 314.1 %all-reduce.15.cloned.1.call-done = (f32[1024,256]{1,0:T(8,128)}, f32[3,3,512,256]{3,2,1,0:T(8,128)}, f32[512,1024]{1,0:T(8,128)}, f32[1024,1024]{1,0:T(8,128)},...) async-done(((f32[1024,256]{1,0:T(8,128)}, f32[3,3,512,256]{3,2,1,0:T(8,128)}, f32[512,1024]{1,0:T(8,128)}, f32[1024,1024]{1,0:T(8,128)}, ...) | async-done | bytes 20971536 | tf_op jit(solution)/shard_map/psum | solution.py:217
  (448 shorter events, 474.2 us)
Async XLA Ops:
  7.2 324.7 %copy-start = (bf16[1024,1024]{1,0:T(8,128)(2,1)S(1)}, bf16[1024,1024]{1,0:T(8,128)(2,1)}, u32[]{:S(2)}) copy-start(bf16[1024,1024]{1,0:T(8,128)(2,1)} %param.41) | copy-start | bytes 6291460
  7.2 17.5 all-gather.4.cloned.1.call-start
  10.9 109.6 %all-gather.6.cloned.1.call-start = ((), (), s32[]{:S(2)}) async-start(), calls=%async_computation.7 | async-start | bytes 1769472 | tf_op jit(solution)/shard_map/all_gather | solution.py:23
  11.7 96.4 %copy-start.60 = (f32[1,256]{1,0:T(1,128)}, f32[1,256]{1,0:T(1,128)S(1)}, u32[]{:S(2)}) copy-start(f32[1,256]{1,0:T(1,128)S(1)} %get-tuple-element.278) | copy-start | bytes 3076
  11.7 96.4 %copy-start.62 = (f32[1,256]{1,0:T(1,128)}, f32[1,256]{1,0:T(1,128)S(1)}, u32[]{:S(2)}) copy-start(f32[1,256]{1,0:T(1,128)S(1)} %get-tuple-element.279) | copy-start | bytes 3076
  27.3 82.0 %copy-start.2 = (f32[2,18,32,256]{3,2,1,0:T(8,128)}, f32[2,18,32,256]{3,2,1,0:T(8,128)S(1)}, u32[]{:S(2)}) copy-start(f32[2,18,32,256]{3,2,1,0:T(8,128)S(1)} %get-tuple-element.296) | copy-start | bytes 3538948
  109.4 312.5 %all-gather.8.cloned.1.call-start = ((), (), s32[]{:S(2)}) async-start(), calls=%async_computation.8 | async-start | bytes 1769472 | tf_op jit(solution)/shard_map/all_gather | solution.py:23
  110.1 178.5 %copy-start.68 = (f32[1,256]{1,0:T(1,128)}, f32[1,256]{1,0:T(1,128)S(1)}, u32[]{:S(2)}) copy-start(f32[1,256]{1,0:T(1,128)S(1)} %get-tuple-element.276) | copy-start | bytes 3076
  110.1 178.5 %copy-start.70 = (f32[1,256]{1,0:T(1,128)}, f32[1,256]{1,0:T(1,128)S(1)}, u32[]{:S(2)}) copy-start(f32[1,256]{1,0:T(1,128)S(1)} %get-tuple-element.277) | copy-start | bytes 3076
  170.5 39.1 %copy-start.38 = (bf16[2,9,16,512]{3,2,1,0:T(8,128)(2,1)}, bf16[2,9,16,512]{3,2,1,0:T(8,128)(2,1)S(1)}, u32[]{:S(2)}) copy-start(bf16[2,9,16,512]{3,2,1,0:T(8,128)(2,1)S(1)} %slice.533) | copy-start | bytes 884740
  179.0 30.8 %copy-start.36 = (bf16[2,9,16,512]{3,2,1,0:T(8,128)(2,1)}, bf16[2,9,16,512]{3,2,1,0:T(8,128)(2,1)S(1)}, u32[]{:S(2)}) copy-start(bf16[2,9,16,512]{3,2,1,0:T(8,128)(2,1)S(1)} %slice.535) | copy-start | bytes 884740
  187.1 23.0 copy-start.34
  195.1 15.3 copy-start.32
  211.3 77.4 %copy-start.16 = (f32[2,9,16,256]{3,2,1,0:T(8,128)}, f32[2,9,16,256]{3,2,1,0:T(8,128)S(1)}, u32[]{:S(2)}) copy-start(f32[2,9,16,256]{3,2,1,0:T(8,128)S(1)} %get-tuple-element.298) | copy-start | bytes 884740
  292.6 121.2 %copy-start.4 = (f32[2,9,16,1024]{3,2,1,0:T(8,128)}, f32[2,9,16,1024]{3,2,1,0:T(8,128)S(1)}, u32[]{:S(2)}) copy-start(f32[2,9,16,1024]{3,2,1,0:T(8,128)S(1)} %get-tuple-element.300) | copy-start | bytes 3538948
  416.6 304.7 %reduce-scatter.11.cloned.1.call-start = ((), (), s32[]{:S(2)}) async-start(), calls=%async_computation.9 | async-start | bytes 442368 | tf_op jit(solution)/shard_map/reduce_scatter | solution.py:27
  416.7 87.2 %copy-start.80 = (f32[1,256]{1,0:T(1,128)}, f32[1,256]{1,0:T(1,128)S(1)}, u32[]{:S(2)}) copy-start(f32[1,256]{1,0:T(1,128)S(1)} %get-tuple-element.274) | copy-start | bytes 3076
  416.7 87.2 %copy-start.82 = (f32[1,256]{1,0:T(1,128)}, f32[1,256]{1,0:T(1,128)S(1)}, u32[]{:S(2)}) copy-start(f32[1,256]{1,0:T(1,128)S(1)} %get-tuple-element.275) | copy-start | bytes 3076
  423.9 80.0 %copy-start.21 = (f32[2,9,16,256]{3,2,1,0:T(8,128)}, f32[2,9,16,256]{3,2,1,0:T(8,128)S(1)}, u32[]{:S(2)}) copy-start(f32[2,9,16,256]{3,2,1,0:T(8,128)S(1)} %get-tuple-element.303) | copy-start | bytes 884740
  466.6 42.1 %copy-start.64 = (f32[256]{0:T(256)}, f32[256]{0:T(256)S(1)}, u32[]{:S(2)}) copy-start(f32[256]{0:T(256)S(1)} %broadcast_divide_fusion.4) | copy-start | bytes 3076
  592.6 78.2 %copy-start.18 = (bf16[2,9,16,1024]{3,2,1,0:T(8,128)(2,1)S(1)}, bf16[2,9,16,1024]{3,2,1,0:T(8,128)(2,1)}, u32[]{:S(2)}) copy-start(bf16[2,9,16,1024]{3,2,1,0:T(8,128)(2,1)} %multiply_convert_fusion.6) | copy-start | bytes 1769476
  717.6 102.3 %reduce-scatter.13.cloned.1.call-start = ((), (), s32[]{:S(2)}) async-start(), calls=%async_computation.10 | async-start | bytes 442368 | tf_op jit(solution)/shard_map/reduce_scatter | solution.py:27
  816.2 55.3 %reduce-scatter.15.cloned.1.call-start = ((), (), s32[]{:S(2)}) async-start(), calls=%async_computation.11 | async-start | bytes 1769472 | tf_op jit(solution)/shard_map/reduce_scatter | solution.py:27
  866.8 60.5 %reduce-scatter.17.cloned.1.call-start = ((), (), s32[]{:S(2)}) async-start(), calls=%async_computation.12 | async-start | bytes 442368 | tf_op jit(solution)/shard_map/reduce_scatter | solution.py:27
  923.0 421.3 %reduce-scatter.19.cloned.1.call-start = ((), (), s32[]{:S(2)}) async-start(), calls=%async_computation.13 | async-start | bytes 1769472
  1333.3 559.7 %reduce-scatter.21.cloned.1.call-start = ((), (), s32[]{:S(2)}) async-start(), calls=%async_computation.14 | async-start | bytes 3538944
  1427.1 36.6 %copy-start.3 = (f32[2,18,32,256]{3,2,1,0:T(8,128)S(1)}, f32[2,18,32,256]{3,2,1,0:T(8,128)}, u32[]{:S(2)}) copy-start(f32[2,18,32,256]{3,2,1,0:T(8,128)} %copy-done.2) | copy-start | bytes 3538948
  1427.1 36.6 %copy-start.59 = (f32[256]{0:T(256)S(1)}, f32[256]{0:T(256)}, u32[]{:S(2)}) copy-start(f32[256]{0:T(256)} %copy-done.58) | copy-start | bytes 3076
  1427.1 36.6 %copy-start.61 = (f32[1,256]{1,0:T(1,128)S(1)}, f32[1,256]{1,0:T(1,128)}, u32[]{:S(2)}) copy-start(f32[1,256]{1,0:T(1,128)} %copy-done.60) | copy-start | bytes 3076
  1427.1 36.6 %copy-start.63 = (f32[1,256]{1,0:T(1,128)S(1)}, f32[1,256]{1,0:T(1,128)}, u32[]{:S(2)}) copy-start(f32[1,256]{1,0:T(1,128)} %copy-done.62) | copy-start | bytes 3076
  1866.9 579.5 %all-reduce.15.cloned.1.call-start = ((), (), s32[]{:S(2)}) async-start(), calls=%async_computation.15 | async-start | bytes 41943040 | tf_op jit(solution)/shard_map/psum | solution.py:217
  2453.7 6.4 slice-start
  (85 other events, 211.1 us)
Sparse Core Ops, SparseCore 0:
  11.0 13.6 all-gather.3
  109.5 6.9 all-gather.5
  416.7 5.0 all-gather.7
  717.7 3.5 reduce-scatter.10
  816.3 3.5 reduce-scatter.12
  866.9 4.5 reduce-scatter.14
  923.2 3.5 reduce-scatter.16
  1333.4 4.5 reduce-scatter.18
  1867.0 7.6 reduce-scatter.20
  1888.9 557.4 all-reduce.14
where the time goes:
time: 2500 us; the launch traced here: 2470 us
  local copies, waits for them, and re-layouts  1030 us (41%)
  blocking collectives  749 us (30%)
  waiting for transfers between devices  342 us (14%)
  other arithmetic  254 us (10%)
  matrix products  79.8 us (3%)
    unnamed x229, local copies, waits for them, and re-layouts  841 us
    psum x1, waiting for transfers between devices, local(): lax.psum((reduce1_grad, spatial1_grad, expand1_grad, shortcut_grad, reduc...  314 us
    psum x7, blocking collectives, normalize(): totals, pixels = lax.psum((first[0], first[1]), 'dp')  276 us
    psum x6, blocking collectives, norm_back(): beta_grad, gamma_grad = lax.psum((local_sums[0], local_sums[1]), 'dp')  244 us
    psum x6, blocking collectives, normalize(): spread = lax.psum(second, 'dp')  222 us
    scatter-add x9, other arithmetic, spatial_back(): input_part = input_part.at[:, row_slice, col_slice, :].add(contribution)  175 us
    slice x10, local copies, waits for them, and re-layouts, spatial(): window = padded[:, row_slice, col_slice, :]  81.9 us
  transfers between devices with their start and end apart: 10, of which 6 were waited for; matrix products, arithmetic and copies ran while one was open for 12% of the time, Pallas kernels for 0%

commit v1 on v0

v1 whole, which is shorter than its diff:
```python
import jax
import jax.numpy as jnp
from jax import lax
from jax.sharding import PartitionSpec as P

epsilon = 1e-05
f32 = jnp.float32
bf16 = jnp.bfloat16
SWAP = [(0, 1), (1, 0)]


def swap(value):
    return lax.ppermute(value, "chan", SWAP)


def in_order(core, own, other, axis=-1):
    return jnp.where(
        core == 0,
        jnp.concatenate([own, other], axis),
        jnp.concatenate([other, own], axis),
    )


def part_of(value, index, axis=-1):
    axis = axis % value.ndim
    size = value.shape[axis] // 2
    return lax.dynamic_slice_in_dim(value, index * size, size, axis)


def exchange(local, count):
    spread = jnp.broadcast_to(local[None], (count,) + local.shape)
    return lax.all_to_all(spread, "dp", 0, 0, tiled=True)


def matmul(left, right):
    return lax.dot_general(left, right, (((1,), (0,)), ((), ())), preferred_element_type=f32)


def matmul_nt(left, right):
    return lax.dot_general(left, right, (((1,), (1,)), ((), ())), preferred_element_type=f32)


def matmul_tn(left, right):
    return lax.dot_general(left, right, (((0,), (0,)), ((), ())), preferred_element_type=f32)


def local_stats(values, mask, cells):
    total = jnp.sum(values * mask, axis=0)
    centred = values - total / cells
    return jnp.stack([total, jnp.sum(centred * centred * mask, axis=0)])


def moments(gathered, cells_each, pixels):
    totals, squares = gathered[:, 0], gathered[:, 1]
    average = jnp.sum(totals, axis=0) / pixels
    offsets = totals / cells_each[:, None] - average
    variance = (jnp.sum(squares, axis=0) + jnp.sum(cells_each[:, None] * offsets * offsets, axis=0)) / pixels
    return average, lax.rsqrt(variance + epsilon)


def silu_slope(values):
    logistic = jax.nn.sigmoid(values)
    return logistic * (1.0 + values * (1.0 - logistic))


def shifted(values, rows, cols):
    height, width = values.shape[1:3]
    padded = jnp.pad(values, ((0, 0), (1, 1), (1, 1), (0, 0)))
    return padded[:, 1 + rows : 1 + rows + height, 1 + cols : 1 + cols + width, :]


def solution(mesh):
    count = mesh.shape["dp"]

    def local(images, extents, cotangent, reduce1, spatial1, expand1, shortcut, reduce2, spatial2, expand2,
              norm_one, norm_two, norm_three, norm_skip, norm_four, norm_five, norm_six):
        core = lax.axis_index("chan")
        imgs, height, width = cotangent.shape[:3]
        grid = height * width
        outer = imgs * grid
        cid = images.shape[3]
        mid = reduce1.shape[1]

        cell = lax.broadcasted_iota(jnp.int32, (imgs, grid), 1)
        valid = (cell // width < extents[:, 0:1]) & (cell % width < extents[:, 1:2])
        mask = valid.astype(f32).reshape(outer, 1)
        mask4 = jnp.tile(mask, (4, 1))
        cells = jnp.sum(extents[:, 0] * extents[:, 1]).astype(f32)

        target = lax.broadcasted_iota(jnp.int32, (4 * grid, 4 * grid), 0)
        source = lax.broadcasted_iota(jnp.int32, (4 * grid, 4 * grid), 1)
        plane, place = target // grid, target % grid
        place = (2 * (place // width) + plane // 2) * 2 * width + 2 * (place % width) + plane % 2
        pick = (source == place).astype(bf16)
        flat = images.reshape(imgs, 4 * grid, cid)
        sorted_x = [matmul(pick, flat[n]).astype(bf16).reshape(4, 1, grid, cid) for n in range(imgs)]
        own_x = (jnp.concatenate(sorted_x, axis=1).reshape(4 * outer, cid) * mask4.astype(bf16))
        all_x = in_order(core, own_x, swap(own_x))

        def activate(pre, cell_mask):
            return (jax.nn.silu(pre) * cell_mask).astype(bf16)

        def gather(own):
            return in_order(core, own, swap(own))

        conv_one = matmul(all_x, reduce1)
        stats_one = local_stats(conv_one, mask4, 4 * cells)
        got_one = exchange(jnp.concatenate([stats_one, jnp.full((1, mid), cells)]), count)
        cells_each = got_one[:, 2, 0]
        pixels = jnp.sum(cells_each)
        conv_skip = matmul(all_x[:outer], shortcut)
        stats_skip = local_stats(conv_skip, mask, cells)
        mean_one, inv_one = moments(got_one, 4 * cells_each, 4 * pixels)
        hat_one = (conv_one - mean_one) * inv_one
        pre_one = norm_one[0] * hat_one + norm_one[1]
        act_one = gather(activate(pre_one, mask4))

        planes = act_one.reshape(4, imgs, height, width, 2 * mid)
        taps = []
        for r in range(3):
            for s in range(3):
                which = (2 if r != 1 else 0) + (1 if s != 1 else 0)
                taps.append(shifted(planes[which], -1 if r == 0 else 0, -1 if s == 0 else 0).reshape(outer, 2 * mid))
        taps_one = jnp.concatenate(taps, axis=1)
        conv_two = matmul(taps_one, spatial1.reshape(18 * mid, mid))
        got_two = exchange(jnp.concatenate([local_stats(conv_two, mask, cells), stats_skip], axis=1), count)
        mean_two, inv_two = moments(got_two[:, :, :mid], cells_each, pixels)
        hat_two = (conv_two - mean_two) * inv_two
        pre_two = norm_two[0] * hat_two + norm_two[1]
        act_two = gather(activate(pre_two, mask))

        conv_three = matmul(act_two, expand1)
        got_three = exchange(local_stats(conv_three, mask, cells), count)
        mean_skip, inv_skip = moments(got_two[:, :, mid:], cells_each, pixels)
        hat_skip = (conv_skip - mean_skip) * inv_skip
        pre_skip = norm_skip[0] * hat_skip + norm_skip[1]
        mean_three, inv_three = moments(got_three, cells_each, pixels)
        hat_three = (conv_three - mean_three) * inv_three
        joined_one = norm_three[0] * hat_three + norm_three[1] + pre_skip
        block_one = activate(joined_one, mask)
        all_block = gather(block_one)

        conv_four = matmul(all_block, reduce2)
        mean_four, inv_four = moments(exchange(local_stats(conv_four, mask, cells), count), cells_each, pixels)
        hat_four = (conv_four - mean_four) * inv_four
        pre_four = norm_four[0] * hat_four + norm_four[1]
        act_four = gather(activate(pre_four, mask))

        grid_four = act_four.reshape(imgs, height, width, 2 * mid)
        taps_four = jnp.concatenate(
            [shifted(grid_four, r - 1, s - 1).reshape(outer, 2 * mid) for r in range(3) for s in range(3)], axis=1)
        conv_five = matmul(taps_four, spatial2.reshape(18 * mid, mid))
        mean_five, inv_five = moments(exchange(local_stats(conv_five, mask, cells), count), cells_each, pixels)
        hat_five = (conv_five - mean_five) * inv_five
        pre_five = norm_five[0] * hat_five + norm_five[1]
        act_five = gather(activate(pre_five, mask))

        conv_six = matmul(act_five, expand2)
        mean_six, inv_six = moments(exchange(local_stats(conv_six, mask, cells), count), cells_each, pixels)
        hat_six = (conv_six - mean_six) * inv_six
        joined_two = norm_six[0] * hat_six + norm_six[1] + block_one.astype(f32)
        block_two = activate(joined_two, mask)

        grad_join2 = cotangent.reshape(outer, -1).astype(f32) * mask * silu_slope(joined_two)

        def norm_sums(grad, *hats):
            local_sums = jnp.stack([jnp.sum(grad, axis=0)] + [jnp.sum(grad * hat, axis=0) for hat in hats])
            return jnp.sum(exchange(local_sums, count), axis=0)

        def norm_back(grad, hat, inv, beta_grad, gamma_grad, norm, cell_mask, total):
            out = cell_mask * norm[0] * inv * (grad - (beta_grad + hat * gamma_grad) / total)
            return out.astype(bf16), jnp.stack([gamma_grad, beta_grad])

        def spread_out(own_part, other_part):
            return own_part + swap(other_part.astype(bf16)).astype(f32)

        def back_1x1(grad, weight):
            return spread_out(matmul_nt(grad, part_of(weight, core, 0)),
                              matmul_nt(grad, part_of(weight, 1 - core, 0)))

        sums = norm_sums(grad_join2, hat_six)
        grad_six, norm_six_grad = norm_back(grad_join2, hat_six, inv_six, sums[0], sums[1], norm_six, mask, pixels)
        expand2_grad = matmul_tn(act_five, grad_six)
        pre_grad = back_1x1(grad_six, expand2) * mask * silu_slope(pre_five)
        sums = norm_sums(pre_grad, hat_five)
        grad_five, norm_five_grad = norm_back(pre_grad, hat_five, inv_five, sums[0], sums[1], norm_five, mask, pixels)

        def shifts_of(grad, choices):
            cube = grad.reshape(imgs, height, width, -1)
            return [shifted(cube, i, j).reshape(outer, -1) for i, j in choices]

        def kernel_rows(kernel, index):
            return part_of(kernel, index, 2)

        moved = shifts_of(grad_five, [(1 - r, 1 - s) for r in range(3) for s in range(3)])
        moved_five = jnp.concatenate(moved, axis=1)
        spatial2_grad = matmul_tn(act_four, moved_five).reshape(2 * mid, 9, mid).transpose(1, 0, 2).reshape(3, 3, 2 * mid, mid)

        def back_five(index):
            rows = kernel_rows(spatial2, index)
            return sum(matmul_nt(moved[3 * r + s], rows[r, s]) for r in range(3) for s in range(3))

        pre_grad = spread_out(back_five(core), back_five(1 - core)) * mask * silu_slope(pre_four)
        sums = norm_sums(pre_grad, hat_four)
        grad_four, norm_four_grad = norm_back(pre_grad, hat_four, inv_four, sums[0], sums[1], norm_four, mask, pixels)
        reduce2_grad = matmul_tn(all_block, grad_four)
        grad_join1 = (grad_join2 + back_1x1(grad_four, reduce2)) * mask * silu_slope(joined_one)

        sums = norm_sums(grad_join1, hat_three, hat_skip)
        grad_three, norm_three_grad = norm_back(grad_join1, hat_three, inv_three, sums[0], sums[1], norm_three, mask, pixels)
        grad_skip, norm_skip_grad = norm_back(grad_join1, hat_skip, inv_skip, sums[0], sums[2], norm_skip, mask, pixels)
        expand1_grad = matmul_tn(act_two, grad_three)
        shortcut_grad = matmul_tn(all_x[:outer], grad_skip)
        pre_grad = back_1x1(grad_three, expand1) * mask * silu_slope(pre_two)
        sums = norm_sums(pre_grad, hat_two)
        grad_two, norm_two_grad = norm_back(pre_grad, hat_two, inv_two, sums[0], sums[1], norm_two, mask, pixels)

        g00, g01, g10, g11 = shifts_of(grad_two, [(0, 0), (0, 1), (1, 0), (1, 1)])
        act_planes = act_one.reshape(4, outer, 2 * mid)
        uses = {(1, 1): (0, g00), (1, 2): (1, g00), (1, 0): (1, g01), (2, 1): (2, g00), (0, 1): (2, g10),
                (2, 2): (3, g00), (2, 0): (3, g01), (0, 2): (3, g10), (0, 0): (3, g11)}
        spatial1_grad = jnp.stack([
            jnp.stack([matmul_tn(act_planes[uses[r, s][0]], uses[r, s][1]) for s in range(3)]) for r in range(3)])

        def back_two(index):
            rows = kernel_rows(spatial1, index)
            out = [0.0] * 4
            for (r, s), (which, grad) in uses.items():
                out[which] = out[which] + matmul_nt(grad, rows[r, s])
            return jnp.concatenate(out, axis=0)

        pre_grad = spread_out(back_two(core), back_two(1 - core)) * mask4 * silu_slope(pre_one)
        sums = norm_sums(pre_grad, hat_one)
        grad_one, norm_one_grad = norm_back(pre_grad, hat_one, inv_one, sums[0], sums[1], norm_one, mask4, 4 * pixels)
        reduce1_grad = matmul_tn(all_x, grad_one)

        def back_x(index):
            part = matmul_nt(grad_one, part_of(reduce1, index, 0))
            skip = matmul_nt(grad_skip, part_of(shortcut, index, 0))
            return jnp.concatenate([part[:outer] + skip, part[outer:]], axis=0)

        grad_x = (spread_out(back_x(core), back_x(1 - core)) * mask4).astype(bf16).reshape(4, imgs, grid, cid)
        input_grad = jnp.stack([matmul_tn(pick, grad_x[:, n].reshape(4 * grid, cid)).astype(bf16) for n in range(imgs)])

        grads = (reduce1_grad, spatial1_grad, expand1_grad, shortcut_grad, reduce2_grad, spatial2_grad, expand2_grad)
        grads = tuple(lax.psum(g.astype(bf16), "dp").astype(f32) for g in grads)
        return (block_one.reshape(cotangent.shape), block_two.reshape(cotangent.shape), input_grad.reshape(images.shape),
                *grads, norm_one_grad, norm_two_grad, norm_three_grad, norm_skip_grad, norm_four_grad, norm_five_grad,
                norm_six_grad)

    wide = P("dp", None, None, "chan")
    weights = (P(None, "chan"), P(None, None, None, "chan")) + (P(None, "chan"),) * 3 + (P(None, None, None, "chan"), P(None, "chan"))
    norms = (P(None, "chan"),) * 7
    return jax.shard_map(
        local, mesh=mesh,
        in_specs=(wide, P("dp", None), wide) + weights + norms,
        out_specs=(wide, wide, wide) + weights + norms,
        check_vma=False)
```

time: 2500 us -> 653 us (0.26)
  local copies, waits for them, and re-layouts: 1030 us -> 60.3 us
  blocking collectives: 749 us -> 0 us
  other arithmetic: 254 us -> 81.3 us
  starting transfers between devices: 0.41 us -> 57.6 us
    unnamed x229 -> x293, local copies, waits for them, and re-layouts: 841 us -> 27.4 us
    psum x19 -> x0, blocking collectives: 743 us -> none  [the longest x7 276 us: normalize(): totals, pixels = lax.psum((first[0], first[1]), 'dp')]
    scatter-add x10 -> x0, other arithmetic: 196 us -> none  [the longest x9 175 us: spatial_back(): input_part = input_part.at[:, row_slice, col_slice, :].add(contribution)]
    slice x21 -> x25, local copies, waits for them, and re-layouts: 97.8 us -> 14.5 us  [the longest x5 1.56 us: local(): sums[0]]
    all_to_all x0 -> x12, waiting for transfers between devices: none -> 63.3 us  [exchange(): return lax.all_to_all(spread, 'dp', 0, 0, tiled=True)]
    all_to_all x0 -> x12, starting transfers between devices: none -> 55.6 us  [exchange(): return lax.all_to_all(spread, 'dp', 0, 0, tiled=True)]
    reduce_scatter x1 -> x0, local copies, waits for them, and re-layouts: 36.6 us -> none  [spread_out(): lax.psum_scatter(partial_sums.astype(jnp.bfloat16), 'chan', scatter_dimen...]
    scatter-add x7 -> x0, local copies, waits for them, and re-layouts: 29.4 us -> none  [spatial_back(): input_part = input_part.at[:, row_slice, col_slice, :].add(contribution)]
  transfers between devices with their start and end apart: 10 -> 25, of which waited for: 6 -> 17; matrix products, arithmetic and copies ran while one was open for 12% -> 11% of each run, Pallas kernels for 0% -> 0%
where the time goes in v1:
time: 653 us; the launch traced here: 642 us
  waiting for transfers between devices  363 us (56%)
  other arithmetic  81.3 us (12%)
  matrix products  62 us (9%)
  local copies, waits for them, and re-layouts  60.3 us (9%)
  starting transfers between devices  57.6 us (9%)
  between operations  18.3 us (3%)
    psum x1, waiting for transfers between devices, local(): grads = tuple((lax.psum(g.astype(bf16), 'dp').astype(f32) for g in grads))  292 us
    all_to_all x12, waiting for transfers between devices, exchange(): return lax.all_to_all(spread, 'dp', 0, 0, tiled=True)  63.3 us
    all_to_all x12, starting transfers between devices, exchange(): return lax.all_to_all(spread, 'dp', 0, 0, tiled=True)  55.6 us
    unnamed x293, local copies, waits for them, and re-layouts  27.4 us
    dot_general x17, matrix products, matmul_tn(): lax.dot_general(left, right, (((0,), (0,)), ((), ())), preferred_element_...  25 us
    dot_general x46, matrix products, matmul_nt(): lax.dot_general(left, right, (((1,), (1,)), ((), ())), preferred_element_...  23.2 us
    convert_element_type x7, other arithmetic, local(): grads = tuple((lax.psum(g.astype(bf16), 'dp').astype(f32) for g in grads))  16.2 us
    dot_general x9, matrix products, matmul(): lax.dot_general(left, right, (((1,), (0,)), ((), ())), preferred_element_...  13.8 us
  transfers between devices with their start and end apart: 25, of which 17 were waited for; matrix products, arithmetic and copies ran while one was open for 11% of the time, Pallas kernels for 0%

profile of v1, /device:TPU:0, one launch (start us, length us, event | category | flops | bytes accessed | tf_op | source)
XLA Modules:
  0.0 642.0 jit_solution(4109575242978525506)
XLA Ops:
  25.1 8.3 %all-to-all-start = ((f32[16,3,256]{2,1,0:T(4,128)}), f32[16,3,256]{2,1,0:T(4,128)}, u32[]{:S(2)}, u32[]{:S(2)}) async-start(f32[16,3,256]{2,1,0:T(4,128)} %broadcast_in_dim.29), calls=%async_computation | async-start | bytes 131072 | tf_op jit(solution)/shard_map/all_to_all | solution.py:32
  33.9 7.0 %all-to-all-done = f32[16,3,256]{2,1,0:T(4,128)} async-done(((f32[16,3,256]{2,1,0:T(4,128)}), f32[16,3,256]{2,1,0:T(4,128)}, u32[]{:S(2)}, u32[]{:S(2)}) %all-to-all-start) | async-done | bytes 49184 | tf_op jit(solution)/shard_map/all_to_all | solution.py:32
  54.1 4.2 all-to-all-start.1
  60.9 5.9 all-to-all-done.1
  75.3 4.2 all-to-all-start.2
  82.4 5.4 all-to-all-done.2
  99.1 4.3 all-to-all-start.3
  104.8 6.0 all-to-all-done.3
  118.8 4.1 all-to-all-start.4
  124.2 6.1 all-to-all-done.4
  138.7 4.2 all-to-all-start.5
  144.3 6.7 %all-to-all-done.5 = f32[16,2,1024]{2,1,0:T(2,128)} async-done(((f32[16,2,1024]{2,1,0:T(2,128)}), f32[16,2,1024]{2,1,0:T(2,128)}, u32[]{:S(2)}, u32[]{:S(2)}) %all-to-all-start.5) | async-done | bytes 131104 | tf_op jit(solution)/shard_map/all_to_all | solution.py:32
  154.0 3.7 fusion.171
  158.4 4.2 all-to-all-start.6
  162.6 7.8 %all-to-all-done.6 = f32[16,2,1024]{2,1,0:T(2,128)} async-done(((f32[16,2,1024]{2,1,0:T(2,128)}), f32[16,2,1024]{2,1,0:T(2,128)}, u32[]{:S(2)}, u32[]{:S(2)}) %all-to-all-start.6) | async-done | bytes 131104 | tf_op jit(solution)/shard_map/all_to_all | solution.py:32
  182.2 4.1 all-to-all-start.7
  189.4 4.3 all-to-all-done.7
  205.2 3.5 all-to-all-start.8
  210.2 5.8 all-to-all-done.8
  228.9 3.4 fusion.170
  233.0 4.4 all-to-all-start.9
  237.5 4.5 convolution_convert_fusion
  241.9 4.3 copy.81
  246.2 4.3 copy.82
  250.5 3.4 convolution_convert_fusion.1
  260.2 3.7 convolution_convert_fusion.2
  265.0 6.7 %all-to-all-start.10 = ((f32[16,2,256]{2,1,0:T(2,128)}), f32[16,2,256]{2,1,0:T(2,128)S(1)}, u32[]{:S(2)}, u32[]{:S(2)}) async-start(f32[16,2,256]{2,1,0:T(2,128)} %broadcast_in_dim.40), calls=%async_computation.10 | async-start | bytes 65536 | tf_op jit(solution)/shard_map/all_to_all | solution.py:32
  274.5 4.6 all-to-all-done.10
  294.7 3.5 all-to-all-start.11
  301.8 3.8 all-to-all-done.11
  323.7 292.3 %all-reduce.9.cloned.1.call-done = (bf16[1024,256]{1,0:T(8,128)(2,1)}, bf16[3,3,512,256]{3,2,1,0:T(8,128)(2,1)}, bf16[512,1024]{1,0:T(8,128)(2,1)}, bf16[1024,10...) async-done(((bf16[1024,256]{1,0:T(8,128)(2,1)}, bf16[3,3,512,256]{3,2,1,0:T(8,128)(2,1)}, ...) | async-done | bytes 10485776 | tf_op jit(solution)/shard_map/psum | solution.py:246
  618.0 4.4 convert_element_type.236
  (540 shorter events, 180.9 us)
Async XLA Ops:
  7.2 109.2 %copy-start = (bf16[3,3,512,256]{3,2,1,0:T(8,128)(2,1)S(1)}, bf16[3,3,512,256]{3,2,1,0:T(8,128)(2,1)}, u32[]{:S(2)}) copy-start(bf16[3,3,512,256]{3,2,1,0:T(8,128)(2,1)} %param.25) | copy-start | bytes 7077892
  17.2 3.1 collective-permute-start
  22.7 10.7 %copy-start.123 = (f32[2,256]{1,0:T(2,128)S(1)}, f32[2,256]{1,0:T(2,128)}, u32[]{:S(2)}) copy-start(f32[2,256]{1,0:T(2,128)} %param.27) | copy-start | bytes 6148
  25.1 15.9 %all-to-all-start = ((f32[16,3,256]{2,1,0:T(4,128)}), f32[16,3,256]{2,1,0:T(4,128)}, u32[]{:S(2)}, u32[]{:S(2)}) async-start(f32[16,3,256]{2,1,0:T(4,128)} %broadcast_in_dim.29), calls=%async_computation | async-start | bytes 131072 | tf_op jit(solution)/shard_map/all_to_all | solution.py:32
  42.5 25.8 %copy-start.75 = (f32[16]{0:T(128)}, f32[16]{0:T(128)S(1)}, u32[]{:S(2)}) copy-start(f32[16]{0:T(128)S(1)} %get-tuple-element.38) | copy-start | bytes 196
  45.3 3.9 collective-permute-start.1
  54.1 12.8 %all-to-all-start.1 = ((f32[16,2,1280]{2,1,0:T(2,128)}), f32[16,2,1280]{2,1,0:T(2,128)}, u32[]{:S(2)}, u32[]{:S(2)}) async-start(f32[16,2,1280]{2,1,0:T(2,128)} %broadcast_in_dim.31), calls=%async_computation.1 | async-start | bytes 327680 | tf_op jit(solution)/shard_map/all_to_all | solution.py:32
  70.1 1.5 collective-permute-start.2
  75.3 12.4 %all-to-all-start.2 = ((f32[16,2,1024]{2,1,0:T(2,128)}), f32[16,2,1024]{2,1,0:T(2,128)}, u32[]{:S(2)}, u32[]{:S(2)}) async-start(f32[16,2,1024]{2,1,0:T(2,128)} %broadcast_in_dim.32), calls=%async_computation.2 | async-start | bytes 262144 | tf_op jit(solution)/shard_map/all_to_all | solution.py:32
  82.4 12.3 %copy-start.52 = (f32[1024]{0:T(1024)}, f32[1024]{0:T(1024)S(1)}, u32[]{:S(2)}) copy-start(f32[1024]{0:T(1024)S(1)} %broadcast_divide_fusion.1) | copy-start | bytes 12292
  94.7 2.1 collective-permute-start.3
  94.8 17.5 %copy-start.76 = (f32[16]{0:T(128)S(1)}, f32[16]{0:T(128)}, u32[]{:S(2)}) copy-start(f32[16]{0:T(128)} %copy-done.75) | copy-start | bytes 196
  99.1 11.7 %all-to-all-start.3 = ((f32[16,2,256]{2,1,0:T(2,128)}), f32[16,2,256]{2,1,0:T(2,128)}, u32[]{:S(2)}, u32[]{:S(2)}) async-start(f32[16,2,256]{2,1,0:T(2,128)} %broadcast_in_dim.33), calls=%async_computation.3 | async-start | bytes 65536 | tf_op jit(solution)/shard_map/all_to_all | solution.py:32
  114.1 1.4 collective-permute-start.4
  118.8 11.5 %all-to-all-start.4 = ((f32[16,2,256]{2,1,0:T(2,128)}), f32[16,2,256]{2,1,0:T(2,128)}, u32[]{:S(2)}, u32[]{:S(2)}) async-start(f32[16,2,256]{2,1,0:T(2,128)} %broadcast_in_dim.34), calls=%async_computation.4 | async-start | bytes 65536 | tf_op jit(solution)/shard_map/all_to_all | solution.py:32
  133.6 1.4 collective-permute-start.5
  138.7 12.2 %all-to-all-start.5 = ((f32[16,2,1024]{2,1,0:T(2,128)}), f32[16,2,1024]{2,1,0:T(2,128)}, u32[]{:S(2)}, u32[]{:S(2)}) async-start(f32[16,2,1024]{2,1,0:T(2,128)} %broadcast_in_dim.35), calls=%async_computation.5 | async-start | bytes 262144 | tf_op jit(solution)/shard_map/all_to_all | solution.py:32
  158.4 12.0 %all-to-all-start.6 = ((f32[16,2,1024]{2,1,0:T(2,128)}), f32[16,2,1024]{2,1,0:T(2,128)}, u32[]{:S(2)}, u32[]{:S(2)}) async-start(f32[16,2,1024]{2,1,0:T(2,128)} %broadcast_in_dim.36), calls=%async_computation.6 | async-start | bytes 262144 | tf_op jit(solution)/shard_map/all_to_all | solution.py:32
  177.3 1.7 collective-permute-start.6
  182.2 11.6 %all-to-all-start.7 = ((f32[16,2,256]{2,1,0:T(2,128)}), f32[16,2,256]{2,1,0:T(2,128)}, u32[]{:S(2)}, u32[]{:S(2)}) async-start(f32[16,2,256]{2,1,0:T(2,128)} %broadcast_in_dim.37), calls=%async_computation.7 | async-start | bytes 65536 | tf_op jit(solution)/shard_map/all_to_all | solution.py:32
  200.2 3.2 collective-permute-start.7
  205.2 10.9 %all-to-all-start.8 = ((f32[16,2,256]{2,1,0:T(2,128)}), f32[16,2,256]{2,1,0:T(2,128)S(1)}, u32[]{:S(2)}, u32[]{:S(2)}) async-start(f32[16,2,256]{2,1,0:T(2,128)} %broadcast_in_dim.38), calls=%async_computation.8 | async-start | bytes 65536 | tf_op jit(solution)/shard_map/all_to_all | solution.py:32
  216.6 12.2 %copy-start.13 = (f32[288,1024]{1,0:T(8,128)S(1)}, f32[288,1024]{1,0:T(8,128)}, u32[]{:S(2)}) copy-start(f32[288,1024]{1,0:T(8,128)} %get-tuple-element.58) | copy-start | bytes 3538948
  218.5 10.3 %copy-start.41 = (bf16[288,256]{1,0:T(8,128)(2,1)}, bf16[288,256]{1,0:T(8,128)(2,1)S(1)}, u32[]{:S(2)}) copy-start(bf16[288,256]{1,0:T(8,128)(2,1)S(1)} %multiply_convert_fusion.8) | copy-start | bytes 442372
  220.1 8.7 %collective-permute-start.8 = (bf16[288,1024]{1,0:T(8,128)(2,1)S(1)}, bf16[288,1024]{1,0:T(8,128)(2,1)S(1)}, u32[]{:S(2)}, u32[]{:S(2)}) collective-permute-start(bf16[288,1024]{1,0:T(8,128)(2,1)S(1)} %convolution_convert_fusion.7), channel_id=1, source_target_pairs={{0,1},{1,0},{2,3},{3,2},{4,5},{5,4},{6,7},{7,6},{8,9},{9,8},{10,11... | collective-permute-start | bytes 1769480 | tf_op jit(solution)/shard_map/ppermute | solution.py:13
  233.0 20.9 %all-to-all-start.9 = ((f32[16,3,1024]{2,1,0:T(4,128)}), f32[16,3,1024]{2,1,0:T(4,128)}, u32[]{:S(2)}, u32[]{:S(2)}) async-start(f32[16,3,1024]{2,1,0:T(4,128)} %broadcast_in_dim.39), calls=%async_computation.9 | async-start | bytes 524288 | tf_op jit(solution)/shard_map/all_to_all | solution.py:32
  259.6 4.3 collective-permute-start.9
  265.0 14.1 %all-to-all-start.10 = ((f32[16,2,256]{2,1,0:T(2,128)}), f32[16,2,256]{2,1,0:T(2,128)S(1)}, u32[]{:S(2)}, u32[]{:S(2)}) async-start(f32[16,2,256]{2,1,0:T(2,128)} %broadcast_in_dim.40), calls=%async_computation.10 | async-start | bytes 65536 | tf_op jit(solution)/shard_map/all_to_all | solution.py:32
  289.0 4.2 collective-permute-start.10
  294.7 10.8 %all-to-all-start.11 = ((f32[16,2,256]{2,1,0:T(2,128)}), f32[16,2,256]{2,1,0:T(2,128)S(1)}, u32[]{:S(2)}, u32[]{:S(2)}) async-start(f32[16,2,256]{2,1,0:T(2,128)} %broadcast_in_dim.41), calls=%async_computation.11 | async-start | bytes 65536 | tf_op jit(solution)/shard_map/all_to_all | solution.py:32
  298.2 317.7 %all-reduce.9.cloned.1.call-start = ((), (), s32[]{:S(2)}) async-start(), calls=%async_computation.12 | async-start | bytes 20971520 | tf_op jit(solution)/shard_map/psum | solution.py:246
  312.8 5.9 collective-permute-start.11
  (128 other events, 400.0 us)
Sparse Core Ops, SparseCore 0:
  309.1 306.7 all-reduce.8
